TPU v7x, 256 devices: a whole 4x4x8 slice. The times are simulated.
256 devices in a mesh: tm: 16 (over z, core), row: 16 (over x, y).
Axes of the slice: x: 4, y: 4, z: 8, core: 2. Of those that a mesh axis runs over, the one named last changes fastest.
Arguments:
- hidden_state: bfloat16 [2, 48, 16, 160, 512], P(None, 'tm', 'row'), may hold values from -64 to 64
- grad_out: bfloat16 [2, 48, 16, 160, 512], P(None, 'tm', 'row'), may hold values from -6 to 6
- norm_gain: float32 [512], replicated, may hold values from 0.1 to 1.9
- norm_shift: float32 [512], replicated, may hold values from -4 to 4
- conv_weight: bfloat16 [512, 27, 512], P('row'), may hold values from -0.0546875 to 0.0546875
Outputs:
- grad_hidden: bfloat16 [2, 48, 16, 160, 512], P(None, 'tm', 'row')
All inputs are finite; a program needn't handle non-finite values.
Results may differ from a plain program's by a relative error of at most 0.001.
Values may be sent and summed in bfloat16 or wider, within the bound.
A program may use at most 192 MiB of HBM per device.

v0:
```python
import jax
import jax.numpy as jnp
from jax import lax
from jax.sharding import PartitionSpec as P

GROUPS = 32


def passed_along(value, axis, steps):
    count = lax.axis_size(axis)
    leading, last = (max(0, -steps), min(count, count - steps))
    return lax.ppermute(value, axis, [(source, source + steps) for source in range(leading, last)])


def padded_2(block, sides, width):
    for axis, dim in sides:
        count = lax.axis_size(axis)
        forward = [(i, i + 1) for i in range(count - 1)]
        backward = [(target, source) for source, target in forward]
        low = lax.ppermute(
            lax.slice_in_dim(block, block.shape[dim] - width, None, axis=dim), axis, forward
        )
        high = lax.ppermute(lax.slice_in_dim(block, 0, width, axis=dim), axis, backward)
        block = jnp.concatenate([low, block, high], axis=dim)
    return block


def shards(hidden_state, grad_out, norm_gain, norm_shift, conv_weight):
    hidden_f = hidden_state.astype(jnp.float32)
    clips, frames, rows, width, chan = hidden_f.shape
    per = chan // GROUPS
    count = frames * lax.axis_size("tm") * rows * lax.axis_size("row") * width * per

    def group_sum(value):
        return jnp.sum(value, axis=(1, 2, 3)).reshape(clips, GROUPS, per).sum(-1)

    def spread(stat):
        return jnp.repeat(stat, per, axis=1)[:, None, None, None, :]

    mean = lax.psum(group_sum(hidden_f), ("tm", "row")) / count
    centered = hidden_f - spread(mean)
    variance = lax.psum(group_sum(centered * centered), ("tm", "row")) / count
    rstd = lax.rsqrt(variance + 1e-06)
    normed = centered * spread(rstd)
    pre = normed * norm_gain + norm_shift
    following = passed_along(grad_out[:, :2], "tm", -1)
    extended = jnp.concatenate([grad_out, following], axis=1)
    rimmed = padded_2(extended, (("row", 2),), 1)
    padded = jnp.pad(rimmed, ((0, 0), (0, 0), (0, 0), (1, 1), (0, 0)))
    full_kernel = lax.all_gather(conv_weight, "row", axis=0, tiled=True)
    total = jnp.zeros((clips, frames, rows, width, full_kernel.shape[0]), jnp.float32)
    for kt in range(3):
        for kr in range(3):
            for kw in range(3):
                window = padded[
                    :, 2 - kt : 2 - kt + frames, 2 - kr : 2 - kr + rows, 2 - kw : 2 - kw + width, :
                ]
                total = total + jnp.einsum(
                    "bfrwo,io->bfrwi",
                    window,
                    full_kernel[:, 9 * kt + 3 * kr + kw, :],
                    preferred_element_type=jnp.float32,
                )
    sig = jax.nn.sigmoid(pre)
    slope = sig * (1.0 + pre * (1.0 - sig))
    grad_pre = total * slope * norm_gain
    first_sum, second_sum = lax.psum(
        (group_sum(grad_pre), group_sum(grad_pre * normed)), ("tm", "row")
    )
    first = first_sum / count
    second = second_sum / count
    grad_hidden = spread(rstd) * (grad_pre - spread(first) - normed * spread(second))
    return grad_hidden.astype(jnp.bfloat16)


def solution(mesh):
    return jax.shard_map(
        shards,
        mesh=mesh,
        in_specs=(
            P(None, "tm", "row", None, None),
            P(None, "tm", "row", None, None),
            P(),
            P(),
            P("row", None, None),
        ),
        out_specs=P(None, "tm", "row", None, None),
        check_vma=False,
    )
```

profile of v0, /device:TPU:1, one launch (start us, length us, event | category | flops | bytes accessed | tf_op | source)
XLA Modules:
  0.0 390.0 jit_solution(3871283386164522698)
XLA Ops:
  8.4 5.3 %collective-permute-start = (bf16[2,2,1,160,512]{4,3,1,0,2:T(8,128)(2,1)S(1)}, bf16[2,2,1,160,512]{4,3,1,0,2:T(8,128)(2,1)S(1)}, u32[]{:S(2)}, u32[]{:S(2)}) collective-permute-start(bf16[2,2,1,160,512]{4,3,1,0,2:T(8,128)(2,1)S(1)} %slice.235), channel_id=1, source_target_pairs={{16,0},{32,16},{48,32},{64,48},{80,64},{96,80},{112,96},{128,112},... | collective-permute-start | bytes 1966088 | tf_op jit(solution)/shard_map/ppermute | solution.py:12
  13.7 8.0 %collective-permute-done = bf16[2,2,1,160,512]{4,3,1,0,2:T(8,128)(2,1)S(1)} collective-permute-done((bf16[2,2,1,160,512]{4,3,1,0,2:T(8,128)(2,1)S(1)}, bf16[2,2,1,160,512]{4,3,1,0,2:T(8,128)(2,1)S(1)}, u32[]{:S(2)}, u32[]{:S(2)}) %collective-permute-start) | collective-permute-done | bytes 655392 | tf_op jit(solution)/shard_map/ppermute | solution.py:12
  24.3 5.5 %collective-permute-start.1 = (bf16[2,5,1,160,512]{4,3,1,0,2:T(8,128)(2,1)}, bf16[2,5,1,160,512]{4,3,1,0,2:T(8,128)(2,1)}, u32[]{:S(2)}, u32[]{:S(2)}) collective-permute-start(bf16[2,5,1,160,512]{4,3,1,0,2:T(8,128)(2,1)} %pad_maximum_fusion), channel_id=1, source_target_pairs={{0,1},{1,2},{2,3},{3,4},{4,5},{5,6},{6,7},{7,8},{8,9},{9,10},{10,1... | collective-permute-start | bytes 4915208 | tf_op jit(solution)/shard_map/ppermute | solution.py:20
  30.1 117.8 %psum.28 = f32[2,32]{1,0:T(2,128)S(1)} all-reduce(f32[2,32]{1,0:T(2,128)S(1)} %reduce_sum.73), channel_id=1, replica_groups=mesh['tm'=16,'row'=16] {'tm','row'}, use_global_device_ids=true, to_apply=%region_2.0 | all-reduce | flops 64 | bytes 512 | tf_op jit(solution)/shard_map/psum | solution.py:40
  148.5 72.4 %psum.29 = f32[2,32]{1,0:T(2,128)S(1)} all-reduce(f32[2,32]{1,0:T(2,128)S(1)} %reduce_sum.75), channel_id=1, replica_groups=mesh['tm'=16,'row'=16] {'tm','row'}, use_global_device_ids=true, to_apply=%region_5.0 | all-reduce | flops 64 | bytes 512 | tf_op jit(solution)/shard_map/psum | solution.py:42
  221.2 6.8 %select_maximum_fusion = bf16[2,5,3,162,512]{4,3,1,0,2:T(8,128)(2,1)} fusion(bf16[2,5,1,160,512]{4,3,1,0,2:T(8,128)(2,1)} %collective-permute-done.2, bf16[2,5,1,160,512]{4,3,1,0,2:T(8,128)(2,1)} %collective-permute-done.1, bf16[2,2,1,160,512]{4,3,1,0,2:T(8,128)(2,1)S(1)} %collective-permute-done, bf16[2,3,1,160,512]{4,3,1,0,2:T(8,128)(2,1)S(1)} %bitcast.292), kind=kLoop, calls=%fused_computation.3 | loop fusion | flops 37324800 | bytes 9891840 | tf_op jit(solution)/shard_map/concatenate | solution.py:24
  227.9 3.5 fusion.34
  231.4 4.1 %fusion.42 = f32[2,3,160,512]{3,2,1,0:T(8,128)} fusion(bf16[2,5,1,160,512]{4,3,1,0,2:T(8,128)(2,1)} %collective-permute-done.1, bf16[512,27,512]{2,0,1:T(8,128)(2,1)} %all-gather.2.cloned.1.call-done), kind=kOutput, calls=%fused_computation.61 | convolution fusion | flops 503316480 | bytes 3473408 | tf_op jit(solution)/shard_map/bfrwo,io->bfrwi/dot_general | solution.py:58
  235.5 3.4 fusion.50
  238.9 3.5 fusion.39
  242.4 3.3 fusion.47
  245.7 3.2 fusion.55
  248.9 2.0 fusion.35
  250.9 2.0 fusion.36
  252.9 2.0 fusion.37
  254.9 2.0 fusion.38
  256.9 2.0 fusion.40
  258.9 2.0 fusion.41
  260.9 2.0 fusion.43
  263.0 2.0 fusion.44
  265.0 2.0 fusion.45
  267.0 2.1 fusion.46
  269.0 2.0 fusion.48
  273.0 2.0 fusion.51
  276.9 2.0 fusion.53
  278.9 2.0 fusion.54
  280.9 2.0 fusion.56
  282.9 2.2 fusion.26
  285.2 2.0 fusion.30
  287.2 2.0 fusion.57
  289.1 17.8 %fusion.61 = (f32[2,512]{1,0:T(2,128)S(1)}, f32[2,512]{1,0:T(2,128)S(1)}, f32[2,3,1,160,512]{4,3,1,0,2:T(8,128)S(1)}) fusion(f32[2,512]{1,0:T(2,128)S(1)} %mul.56, f32[2,512]{1,0:T(2,128)S(1)} %sub.26, bf16[2,3,1,160,512]{4,3,2,1,0:T(8,128)(2,1)S(1)} %copy-done, f32[512]{0:T(512)S(1)} %copy-done.3, f32[512]{0:T(512)S(1)} %copy-done.4, ...), kind=kOutput, calls=%fused_computation.125 | convolution fusion | flops 524449792 | bytes 55595008 | tf_op jit(solution)/shard_map/bfrwo,io->bfrwi/dot_general | solution.py:58
  307.3 74.1 %all-reduce.1 = (f32[2,32]{1,0:T(2,128)S(1)}, f32[2,32]{1,0:T(2,128)S(1)}) all-reduce(f32[2,32]{1,0:T(2,128)S(1)} %reduce_sum.79, f32[2,32]{1,0:T(2,128)S(1)} %reduce_sum.77), channel_id=1, replica_groups=mesh['tm'=16,'row'=16] {'tm','row'}, use_global_device_ids=true, to_apply=%region_11.12 | all-reduce | flops 128 | bytes 1024 | tf_op jit(solution)/shard_map/psum | solution.py:67
  (47 shorter events, 11.6 us)
Async XLA Ops:
  6.5 15.2 %copy-start.1 = (bf16[2,3,1,160,512]{4,3,2,1,0:T(8,128)(2,1)S(1)}, bf16[2,3,1,160,512]{4,3,2,1,0:T(8,128)(2,1)}, u32[]{:S(2)}) copy-start(bf16[2,3,1,160,512]{4,3,2,1,0:T(8,128)(2,1)} %param.6) | copy-start | bytes 2949124
  6.5 221.4 %all-gather.2.cloned.1.call-start = ((), (), s32[]{:S(2)}) async-start(), calls=%async_computation | async-start | bytes 15040512 | tf_op jit(solution)/shard_map/all_gather | solution.py:50
  8.4 21.4 %copy-start = (bf16[2,3,1,160,512]{4,3,2,1,0:T(8,128)(2,1)S(1)}, bf16[2,3,1,160,512]{4,3,2,1,0:T(8,128)(2,1)}, u32[]{:S(2)}) copy-start(bf16[2,3,1,160,512]{4,3,2,1,0:T(8,128)(2,1)} %param.5) | copy-start | bytes 2949124
  8.4 13.3 %collective-permute-start = (bf16[2,2,1,160,512]{4,3,1,0,2:T(8,128)(2,1)S(1)}, bf16[2,2,1,160,512]{4,3,1,0,2:T(8,128)(2,1)S(1)}, u32[]{:S(2)}, u32[]{:S(2)}) collective-permute-start(bf16[2,2,1,160,512]{4,3,1,0,2:T(8,128)(2,1)S(1)} %slice.235), channel_id=1, source_target_pairs={{16,0},{32,16},{48,32},{64,48},{80,64},{96,80},{112,96},{128,112},... | collective-permute-start | bytes 1966088 | tf_op jit(solution)/shard_map/ppermute | solution.py:12
  23.0 198.1 %collective-permute-start.2 = (bf16[2,5,1,160,512]{4,3,1,0,2:T(8,128)(2,1)}, bf16[2,5,1,160,512]{4,3,1,0,2:T(8,128)(2,1)}, u32[]{:S(2)}, u32[]{:S(2)}) collective-permute-start(bf16[2,5,1,160,512]{4,3,1,0,2:T(8,128)(2,1)} %pad_maximum_fusion), channel_id=1, source_target_pairs={{1,0},{2,1},{3,2},{4,3},{5,4},{6,5},{7,6},{8,7},{9,8},{10,9},{11,1... | collective-permute-start | bytes 4915208 | tf_op jit(solution)/shard_map/ppermute | solution.py:23
  24.3 196.8 %collective-permute-start.1 = (bf16[2,5,1,160,512]{4,3,1,0,2:T(8,128)(2,1)}, bf16[2,5,1,160,512]{4,3,1,0,2:T(8,128)(2,1)}, u32[]{:S(2)}, u32[]{:S(2)}) collective-permute-start(bf16[2,5,1,160,512]{4,3,1,0,2:T(8,128)(2,1)} %pad_maximum_fusion), channel_id=1, source_target_pairs={{0,1},{1,2},{2,3},{3,4},{4,5},{5,6},{6,7},{7,8},{8,9},{9,10},{10,1... | collective-permute-start | bytes 4915208 | tf_op jit(solution)/shard_map/ppermute | solution.py:20
  227.9 17.7 %copy-start.2 = (bf16[512,27,512]{2,0,1:T(8,128)(2,1)S(1)}, bf16[512,27,512]{2,0,1:T(8,128)(2,1)}, u32[]{:S(2)}) copy-start(bf16[512,27,512]{2,0,1:T(8,128)(2,1)} %all-gather.2.cloned.1.call-done) | copy-start | bytes 42467332
  231.4 17.5 %slice-start = ((s8[5160960]{0:T(1024)(128)(4,1)}), s8[4194304]{0:T(1024)(128)(4,1)S(1)}, s32[]{:S(2)}) async-start(s8[5160960]{0:T(1024)(128)(4,1)} %bitcast.288), calls=%async_computation.1 | async-start | bytes 8388608
  238.9 10.0 %slice-start.1 = ((s8[5160960]{0:T(1024)(128)(4,1)}), s8[966656]{0:T(1024)(128)(4,1)S(1)}, s32[]{:S(2)}) async-start(s8[5160960]{0:T(1024)(128)(4,1)} %bitcast.288), calls=%async_computation.2 | async-start | bytes 1933312
  287.2 2.0 copy-start.3
  287.2 2.0 copy-start.4
Sparse Core Ops, SparseCore 0:
  9.8 141.7 all-gather.1
where the time goes:
time: 391 us; the launch traced here: 390 us
  blocking collectives  264 us (68%)
  matrix products  79 us (20%)
  between operations  13.5 us (3%)
  starting transfers between devices  12 us (3%)
  other arithmetic  10.3 us (3%)
  waiting for transfers between devices  8.76 us (2%)
    psum x1, blocking collectives, shards(): mean = lax.psum(group_sum(hidden_f), ('tm', 'row')) / count  118 us
    dot_general x27, matrix products, shards(): jnp.einsum('bfrwo,io->bfrwi', window, full_kernel[:, 9 * kt + 3 * kr + kw...  79 us
    psum x1, blocking collectives, shards(): lax.psum((group_sum(grad_pre), group_sum(grad_pre * normed)), ('tm', 'row'))  74.1 us
    psum x1, blocking collectives, shards(): variance = lax.psum(group_sum(centered * centered), ('tm', 'row')) / count  72.4 us
    ppermute x1, waiting for transfers between devices, passed_along(): lax.ppermute(value, axis, [(source, source + steps) for source in range(l...  8.04 us
  transfers between devices with their start and end apart: 4, of which 1 were waited for; matrix products, arithmetic and copies ran while one was open for 3% of the time, Pallas kernels for 0%

commit v1 on v0

--- a/solution.py
+++ b/solution.py
@@ -37,7 +37,7 @@
     def spread(stat):
         return jnp.repeat(stat, per, axis=1)[:, None, None, None, :]
 
-    mean = lax.psum(group_sum(hidden_f), ("tm", "row")) / count
+    mean = jnp.sum(lax.all_gather(group_sum(hidden_f), ("tm", "row")), axis=0) / count
     centered = hidden_f - spread(mean)
     variance = lax.psum(group_sum(centered * centered), ("tm", "row")) / count
     rstd = lax.rsqrt(variance + 1e-06)

time: 391 us -> 425 us (1.087)
  blocking collectives: 264 us -> 299 us
    all_gather x0 -> x1, blocking collectives: none -> 147 us  [shards(): lax.all_gather(group_sum(hidden_f), ('tm', 'row'))]
    psum x1 -> x0, blocking collectives: 118 us -> none  [shards(): mean = lax.psum(group_sum(hidden_f), ('tm', 'row')) / count]
    psum x1, blocking collectives: 72.4 us -> 78.4 us  [shards(): variance = lax.psum(group_sum(centered * centered), ('tm', 'row')) / count]
where the time goes in v1:
time: 425 us
  blocking collectives  299 us (70%)
  matrix products  79 us (19%)
  between operations  13.5 us (3%)
  starting transfers between devices  12 us (3%)
  other arithmetic  10.6 us (2%)
  waiting for transfers between devices  8.76 us (2%)
    all_gather x1, blocking collectives, shards(): lax.all_gather(group_sum(hidden_f), ('tm', 'row'))  147 us
    dot_general x27, matrix products, shards(): jnp.einsum('bfrwo,io->bfrwi', window, full_kernel[:, 9 * kt + 3 * kr + kw...  79 us
    psum x1, blocking collectives, shards(): variance = lax.psum(group_sum(centered * centered), ('tm', 'row')) / count  78.4 us
    psum x1, blocking collectives, shards(): lax.psum((group_sum(grad_pre), group_sum(grad_pre * normed)), ('tm', 'row'))  73.4 us
  transfers between devices with their start and end apart: 4, of which 1 were waited for; matrix products, arithmetic and copies ran while one was open for 3% of the time, Pallas kernels for 0%

profile of v1, /device:TPU:1, one launch (start us, length us, event | category | flops | bytes accessed | tf_op | source)
XLA Modules:
  0.0 424.6 jit_solution(13799796884482257106)
XLA Ops:
  8.4 5.3 %collective-permute-start = (bf16[2,2,1,160,512]{4,3,1,0,2:T(8,128)(2,1)S(1)}, bf16[2,2,1,160,512]{4,3,1,0,2:T(8,128)(2,1)S(1)}, u32[]{:S(2)}, u32[]{:S(2)}) collective-permute-start(bf16[2,2,1,160,512]{4,3,1,0,2:T(8,128)(2,1)S(1)} %slice.235), channel_id=1, source_target_pairs={{16,0},{32,16},{48,32},{64,48},{80,64},{96,80},{112,96},{128,112},... | collective-permute-start | bytes 1966088 | tf_op jit(solution)/shard_map/ppermute | solution.py:12
  13.7 8.0 %collective-permute-done = bf16[2,2,1,160,512]{4,3,1,0,2:T(8,128)(2,1)S(1)} collective-permute-done((bf16[2,2,1,160,512]{4,3,1,0,2:T(8,128)(2,1)S(1)}, bf16[2,2,1,160,512]{4,3,1,0,2:T(8,128)(2,1)S(1)}, u32[]{:S(2)}, u32[]{:S(2)}) %collective-permute-start) | collective-permute-done | bytes 655392 | tf_op jit(solution)/shard_map/ppermute | solution.py:12
  24.3 5.5 %collective-permute-start.1 = (bf16[2,5,1,160,512]{4,3,1,0,2:T(8,128)(2,1)}, bf16[2,5,1,160,512]{4,3,1,0,2:T(8,128)(2,1)}, u32[]{:S(2)}, u32[]{:S(2)}) collective-permute-start(bf16[2,5,1,160,512]{4,3,1,0,2:T(8,128)(2,1)} %pad_maximum_fusion), channel_id=1, source_target_pairs={{0,1},{1,2},{2,3},{3,4},{4,5},{5,6},{6,7},{7,8},{8,9},{9,10},{10,1... | collective-permute-start | bytes 4915208 | tf_op jit(solution)/shard_map/ppermute | solution.py:20
  30.1 146.7 %all-gather.1 = f32[256,2,32]{2,1,0:T(2,128)S(1)} all-gather(f32[1,2,32]{2,1,0:T(2,128)S(1)} %bitcast.296), channel_id=2, replica_groups=mesh['tm'=16,'row'=16] {'tm','row'}, dimensions={0}, use_global_device_ids=true | all-gather | bytes 65792 | tf_op jit(solution)/shard_map/all_gather | solution.py:40
  177.8 78.4 %psum.21 = f32[2,32]{1,0:T(2,128)S(1)} all-reduce(f32[2,32]{1,0:T(2,128)S(1)} %reduce_sum.85), channel_id=1, replica_groups=mesh['tm'=16,'row'=16] {'tm','row'}, use_global_device_ids=true, to_apply=%region_5.0 | all-reduce | flops 64 | bytes 512 | tf_op jit(solution)/shard_map/psum | solution.py:42
  256.4 6.8 %select_maximum_fusion = bf16[2,5,3,162,512]{4,3,1,0,2:T(8,128)(2,1)} fusion(bf16[2,5,1,160,512]{4,3,1,0,2:T(8,128)(2,1)} %collective-permute-done.2, bf16[2,5,1,160,512]{4,3,1,0,2:T(8,128)(2,1)} %collective-permute-done.1, bf16[2,2,1,160,512]{4,3,1,0,2:T(8,128)(2,1)S(1)} %collective-permute-done, bf16[2,3,1,160,512]{4,3,1,0,2:T(8,128)(2,1)S(1)} %bitcast.293), kind=kLoop, calls=%fused_computation.3 | loop fusion | flops 37324800 | bytes 9891840 | tf_op jit(solution)/shard_map/concatenate | solution.py:24
  263.2 3.5 fusion.34
  266.7 4.1 fusion.42
  270.8 3.3 fusion.50
  274.2 3.5 fusion.39
  277.6 3.3 fusion.47
  280.9 3.2 fusion.55
  284.1 2.0 fusion.35
  286.1 2.0 fusion.36
  288.1 2.0 fusion.37
  290.1 2.0 fusion.38
  292.1 2.0 fusion.40
  294.2 2.0 fusion.41
  296.2 2.0 fusion.43
  298.2 2.0 fusion.44
  300.2 2.0 fusion.45
  302.2 2.1 fusion.46
  304.3 2.0 fusion.48
  308.2 2.0 fusion.51
  312.2 2.0 fusion.53
  314.2 2.0 fusion.54
  316.2 2.0 fusion.56
  318.2 2.2 fusion.26
  320.4 2.0 fusion.30
  322.4 2.0 fusion.57
  324.4 17.8 %fusion.61 = (f32[2,512]{1,0:T(2,128)S(1)}, f32[2,512]{1,0:T(2,128)S(1)}, f32[2,3,1,160,512]{4,3,1,0,2:T(8,128)S(1)}) fusion(f32[2,512]{1,0:T(2,128)S(1)} %mul.56, f32[2,512]{1,0:T(2,128)S(1)} %sub.26, bf16[2,3,1,160,512]{4,3,2,1,0:T(8,128)(2,1)S(1)} %copy-done, f32[512]{0:T(512)S(1)} %copy-done.3, f32[512]{0:T(512)S(1)} %copy-done.4, ...), kind=kOutput, calls=%fused_computation.125 | convolution fusion | flops 524449792 | bytes 55595008 | tf_op jit(solution)/shard_map/bfrwo,io->bfrwi/dot_general | solution.py:58
  342.6 73.4 %all-reduce.1 = (f32[2,32]{1,0:T(2,128)S(1)}, f32[2,32]{1,0:T(2,128)S(1)}) all-reduce(f32[2,32]{1,0:T(2,128)S(1)} %reduce_sum.89, f32[2,32]{1,0:T(2,128)S(1)} %reduce_sum.87), channel_id=1, replica_groups=mesh['tm'=16,'row'=16] {'tm','row'}, use_global_device_ids=true, to_apply=%region_11.12 | all-reduce | flops 128 | bytes 1024 | tf_op jit(solution)/shard_map/psum | solution.py:67
  (48 shorter events, 11.9 us)
Async XLA Ops:
  6.5 15.2 %copy-start.1 = (bf16[2,3,1,160,512]{4,3,2,1,0:T(8,128)(2,1)S(1)}, bf16[2,3,1,160,512]{4,3,2,1,0:T(8,128)(2,1)}, u32[]{:S(2)}) copy-start(bf16[2,3,1,160,512]{4,3,2,1,0:T(8,128)(2,1)} %param.6) | copy-start | bytes 2949124
  6.5 256.7 %all-gather.4.cloned.1.call-start = ((), (), s32[]{:S(2)}) async-start(), calls=%async_computation | async-start | bytes 15040512 | tf_op jit(solution)/shard_map/all_gather | solution.py:50
  8.4 21.4 %copy-start = (bf16[2,3,1,160,512]{4,3,2,1,0:T(8,128)(2,1)S(1)}, bf16[2,3,1,160,512]{4,3,2,1,0:T(8,128)(2,1)}, u32[]{:S(2)}) copy-start(bf16[2,3,1,160,512]{4,3,2,1,0:T(8,128)(2,1)} %param.5) | copy-start | bytes 2949124
  8.4 13.3 %collective-permute-start = (bf16[2,2,1,160,512]{4,3,1,0,2:T(8,128)(2,1)S(1)}, bf16[2,2,1,160,512]{4,3,1,0,2:T(8,128)(2,1)S(1)}, u32[]{:S(2)}, u32[]{:S(2)}) collective-permute-start(bf16[2,2,1,160,512]{4,3,1,0,2:T(8,128)(2,1)S(1)} %slice.235), channel_id=1, source_target_pairs={{16,0},{32,16},{48,32},{64,48},{80,64},{96,80},{112,96},{128,112},... | collective-permute-start | bytes 1966088 | tf_op jit(solution)/shard_map/ppermute | solution.py:12
  23.0 233.4 %collective-permute-start.2 = (bf16[2,5,1,160,512]{4,3,1,0,2:T(8,128)(2,1)}, bf16[2,5,1,160,512]{4,3,1,0,2:T(8,128)(2,1)}, u32[]{:S(2)}, u32[]{:S(2)}) collective-permute-start(bf16[2,5,1,160,512]{4,3,1,0,2:T(8,128)(2,1)} %pad_maximum_fusion), channel_id=1, source_target_pairs={{1,0},{2,1},{3,2},{4,3},{5,4},{6,5},{7,6},{8,7},{9,8},{10,9},{11,1... | collective-permute-start | bytes 4915208 | tf_op jit(solution)/shard_map/ppermute | solution.py:23
  24.3 232.1 %collective-permute-start.1 = (bf16[2,5,1,160,512]{4,3,1,0,2:T(8,128)(2,1)}, bf16[2,5,1,160,512]{4,3,1,0,2:T(8,128)(2,1)}, u32[]{:S(2)}, u32[]{:S(2)}) collective-permute-start(bf16[2,5,1,160,512]{4,3,1,0,2:T(8,128)(2,1)} %pad_maximum_fusion), channel_id=1, source_target_pairs={{0,1},{1,2},{2,3},{3,4},{4,5},{5,6},{6,7},{7,8},{8,9},{9,10},{10,1... | collective-permute-start | bytes 4915208 | tf_op jit(solution)/shard_map/ppermute | solution.py:20
  263.2 17.7 %copy-start.2 = (bf16[512,27,512]{2,0,1:T(8,128)(2,1)S(1)}, bf16[512,27,512]{2,0,1:T(8,128)(2,1)}, u32[]{:S(2)}) copy-start(bf16[512,27,512]{2,0,1:T(8,128)(2,1)} %all-gather.4.cloned.1.call-done) | copy-start | bytes 42467332
  266.7 17.4 %slice-start = ((s8[5160960]{0:T(1024)(128)(4,1)}), s8[4194304]{0:T(1024)(128)(4,1)S(1)}, s32[]{:S(2)}) async-start(s8[5160960]{0:T(1024)(128)(4,1)} %bitcast.289), calls=%async_computation.1 | async-start | bytes 8388608
  274.2 10.0 %slice-start.1 = ((s8[5160960]{0:T(1024)(128)(4,1)}), s8[966656]{0:T(1024)(128)(4,1)S(1)}, s32[]{:S(2)}) async-start(s8[5160960]{0:T(1024)(128)(4,1)} %bitcast.289), calls=%async_computation.2 | async-start | bytes 1933312
  322.4 2.0 copy-start.3
  322.4 2.0 copy-start.4
Sparse Core Ops, SparseCore 0:
  9.8 140.7 all-gather.3
